TPU v7x, 512 devices: a whole 4x8x8 slice. The times are simulated.
512 devices in a mesh: seq: 64 (over z, y), head: 8 (over x, core).
Axes of the slice: x: 4, y: 8, z: 8, core: 2. Of those that a mesh axis runs over, the one named last changes fastest.
Arguments:
- raw_keys: bfloat16 [2, 65536, 8, 128], P(None, 'seq', 'head'), may hold values from -6 to 6
- raw_values: bfloat16 [2, 65536, 8, 128], P(None, 'seq', 'head'), may hold values from -6 to 6
- phase: int32 [2], replicated, may hold values from 0 to 255, as said below
- ratio: int32 [2, 64], replicated, may hold values from 8 to 32, as said below
- resident_len: int32 [2, 64], replicated, may hold values from 1 to 256, as said below
- beacon_queries: bfloat16 [2, 8192, 8, 8, 128], P(None, 'seq', 'head'), may hold values from -150 to 150
- beacon_wk: bfloat16 [8192, 1024], P('seq', 'head'), may hold values from -0.125 to 0.125
- beacon_wv: bfloat16 [8192, 1024], P('seq', 'head'), may hold values from -0.125 to 0.125
- resident_keys: bfloat16 [2, 16384, 8, 128], P(None, 'seq', 'head'), may hold values from -6 to 6
- resident_values: bfloat16 [2, 16384, 8, 128], P(None, 'seq', 'head'), may hold values from -6 to 6
- decode_queries: bfloat16 [4, 2, 8, 8, 128], P(None, None, 'head'), may hold values from -150 to 150
- out_weight: bfloat16 [8192, 8192], P('head', 'seq'), may hold values from -0.0625 to 0.0625
Outputs:
- beacon_keys: bfloat16 [2, 8192, 8, 128], P(None, 'seq', 'head')
- beacon_values: bfloat16 [2, 8192, 8, 128], P(None, 'seq', 'head')
- projected: bfloat16 [4, 2, 8192], P(None, None, 'seq')
Inputs may be any that keep to these rules, and one draw needn't show every extreme that they name: `phase`: some request has 255. `ratio`: each value is 1024 // 128 times 1, 2 or 4; both ends occur. `resident_len`: some pair has 256.
All inputs are finite; a program needn't handle non-finite values.
Results may differ from a plain program's by a relative error of at most 0.025.
Values may be sent and summed in bfloat16 or wider, within the bound.
No kernel may reach another device: no remote copies, remote signals or barrier semaphores. Data moves between devices by JAX's collectives and lax.ppermute only.
A program may use at most 64 MiB of HBM per device.

v0:
```python
import math
import jax
import jax.numpy as jnp
from jax import lax
from jax.sharding import PartitionSpec as P

G = 8
INTERVAL = 1024
NB = 128
OFF = 256
STEPS = 4
masked_score = -1e30


def shifted(value, axis, steps):
    count = lax.axis_size(axis)
    first, last = (max(0, -steps), min(count, count - steps))
    return lax.ppermute(value, axis, [(source, source + steps) for source in range(first, last)])


def pool_part(queries, key_rows, value_rows, positions, present, reaches):
    inv_root = 1.0 / math.sqrt(queries.shape[-1])

    def per_request(members):
        query_block, key_block, value_block, position_row, present_row, reach_row = members
        scores = (
            jnp.einsum("jkgd,ikd->jkgi", query_block, key_block, preferred_element_type=jnp.float32)
            * inv_root
        )
        allowed = (
            present_row[None, :]
            & (position_row[None, :] >= 0)
            & (position_row[None, :] < INTERVAL)
            & (position_row[None, :] < reach_row[:, None])
        )
        cache_mask = allowed[:, None, None, :]
        row_peak = jnp.max(jnp.where(cache_mask, scores, masked_score), axis=-1)
        weights = jnp.where(cache_mask, jnp.exp(scores - row_peak[..., None]), 0.0)
        weight_sum = jnp.sum(weights, axis=-1)
        weighted = jnp.einsum(
            "jkgi,ikd->jkgd",
            weights.astype(jnp.bfloat16),
            value_block,
            preferred_element_type=jnp.float32,
        )
        return (row_peak, weight_sum, weighted)

    return lax.map(per_request, (queries, key_rows, value_rows, positions, present, reaches))


def body(
    raw_keys,
    raw_values,
    phase,
    ratio,
    resident_len,
    beacon_queries,
    beacon_wk,
    beacon_wv,
    resident_keys,
    resident_values,
    decode_queries,
    out_weight,
):
    requests = raw_keys.shape[0]
    kv_local = raw_keys.shape[2]
    head_dim = raw_keys.shape[3]
    shard_index = lax.axis_index("seq")
    shard_count = lax.axis_size("seq")
    is_first = shard_index == 0
    is_last = shard_index == shard_count - 1
    own_ratio = lax.dynamic_index_in_dim(ratio, shard_index, 1, keepdims=False)
    slot_ids = jnp.arange(NB, dtype=jnp.int32)
    lead_in = jnp.where(is_first, phase, 0)
    reaches = (slot_ids[None, :] + 1) * own_ratio[:, None] + lead_in[:, None]
    tail_keys = raw_keys[:, INTERVAL - OFF :]
    tail_values = raw_values[:, INTERVAL - OFF :]
    own_positions = jnp.arange(INTERVAL, dtype=jnp.int32)[None, :] + phase[:, None]
    rim_ids = jnp.arange(OFF, dtype=jnp.int32)
    rim_positions = rim_ids[None, :] - OFF + phase[:, None]
    near_keys, near_values = shifted((tail_keys, tail_values), "seq", 1)
    key_rows = jnp.concatenate([near_keys, raw_keys], axis=1)
    value_rows = jnp.concatenate([near_values, raw_values], axis=1)
    positions = jnp.concatenate([rim_positions, own_positions], axis=1)
    present = jnp.logical_not(is_first) | (positions >= phase[:, None])
    pooled_parts = pool_part(beacon_queries, key_rows, value_rows, positions, present, reaches)
    pooled = (pooled_parts[2] / pooled_parts[1][..., None]).astype(jnp.bfloat16)
    pooled_flat = pooled.reshape(requests * NB, kv_local * G * head_dim)
    pooled_whole = lax.all_gather(pooled_flat, "head", axis=1, tiled=True)
    key_sum = jnp.dot(
        pooled_whole,
        lax.all_gather(beacon_wk, "seq", axis=0, tiled=True),
        preferred_element_type=jnp.float32,
    )
    value_sum = jnp.dot(
        pooled_whole,
        lax.all_gather(beacon_wv, "seq", axis=0, tiled=True),
        preferred_element_type=jnp.float32,
    )
    made_keys = key_sum
    made_values = value_sum
    made_keys = made_keys.reshape(requests, NB, kv_local, head_dim)
    made_values = made_values.reshape(requests, NB, kv_local, head_dim)
    slot_live = slot_ids[None, :] < (INTERVAL // own_ratio)[:, None]
    beacon_keys = jnp.where(slot_live[:, :, None, None], made_keys, 0.0).astype(jnp.bfloat16)
    beacon_values = jnp.where(slot_live[:, :, None, None], made_values, 0.0).astype(jnp.bfloat16)
    cache_keys = jnp.concatenate([resident_keys, beacon_keys, tail_keys], axis=1)
    cache_values = jnp.concatenate([resident_values, beacon_values, tail_values], axis=1)
    own_len = lax.dynamic_index_in_dim(resident_len, shard_index, 1, keepdims=False)
    resident_ok = jnp.arange(resident_keys.shape[1], dtype=jnp.int32)[None, :] < own_len[:, None]
    leftover_ok = (rim_ids[None, :] >= OFF - phase[:, None]) & is_last
    usable = jnp.concatenate([resident_ok, slot_live, leftover_ok], axis=1)
    inv_root = 1.0 / math.sqrt(head_dim)
    scores = (
        jnp.einsum(
            "srkgd,rikd->rksgi", decode_queries, cache_keys, preferred_element_type=jnp.float32
        )
        * inv_root
    )
    cache_mask = usable[:, None, None, None, :]
    row_peak = jnp.max(jnp.where(cache_mask, scores, masked_score), axis=-1)
    weights = jnp.where(cache_mask, jnp.exp(scores - row_peak[..., None]), 0.0)
    weight_sum = jnp.sum(weights, axis=-1)
    weighted = jnp.einsum(
        "rksgi,rikd->rksgd",
        weights.astype(jnp.bfloat16),
        cache_values,
        preferred_element_type=jnp.float32,
    )
    global_peak = lax.pmax(row_peak, "seq")
    rescale = jnp.exp(row_peak - global_peak)
    total_sum, total_weighted = lax.psum(
        (weight_sum * rescale, weighted * rescale[..., None]), "seq"
    )
    attended = (total_weighted / total_sum[..., None]).astype(jnp.bfloat16)
    attended = jnp.transpose(attended, (2, 0, 1, 3, 4)).reshape(
        STEPS * requests, kv_local * G * head_dim
    )
    partial_value = jnp.dot(attended, out_weight, preferred_element_type=jnp.float32)
    summed = lax.psum(partial_value, "head")
    projected = summed.astype(jnp.bfloat16).reshape(STEPS, requests, out_weight.shape[1])
    return (beacon_keys, beacon_values, projected)


def solution(mesh):
    return jax.shard_map(
        body,
        mesh=mesh,
        in_specs=(
            P(None, "seq", "head", None),
            P(None, "seq", "head", None),
            P(),
            P(),
            P(),
            P(None, "seq", "head", None, None),
            P("seq", "head"),
            P("seq", "head"),
            P(None, "seq", "head", None),
            P(None, "seq", "head", None),
            P(None, None, "head", None, None),
            P("head", "seq"),
        ),
        out_specs=(
            P(None, "seq", "head", None),
            P(None, "seq", "head", None),
            P(None, None, "seq"),
        ),
        check_vma=False,
    )
```

profile of v0, /device:TPU:1, one launch (start us, length us, event | category | flops | bytes accessed | tf_op | source)
XLA Modules:
  0.0 666.6 jit_solution(5328392180371530264)
XLA Ops:
  7.2 0.0 all-gather.6.cloned.1.call-start
  7.2 1.0 slice.9
  8.2 4.7 collective-permute-start.1
  12.9 0.9 slice.8
  13.8 2.6 collective-permute-start
  16.4 0.0 all-gather.6.cloned.1.call-update
  16.4 0.0 all-gather.4.cloned.1.call-start
  16.5 0.7 broadcast_subtract_fusion
  17.2 0.7 iota_add_fusion
  17.9 1.2 copy.32
  19.2 0.7 broadcast_add_fusion
  19.9 0.7 compare_or_fusion
  20.6 1.0 fusion.44
  21.7 0.1 multiply_add_fusion
  21.8 1.1 pad_maximum_fusion
  22.9 1.0 copy.31
  23.9 0.9 pad_maximum_fusion.1
  24.8 8.6 %while.12 = (s32[]{:T(128)}, f32[2,128,1,8]{1,3,2,0:T(8,128)S(1)}, f32[2,128,1,8,128]{1,4,3,2,0:T(8,128)S(1)}, pred[2,1280]{1,0:T(4,128)(4,1)S(1)}, s32[2,1280]{...) while((s32[]{:T(128)}, f32[2,128,1,8]{1,3,2,0:T(8,128)S(1)}, ...), condition=%wide.region_3.4_spmd, body=%wide.region_0.3_spmd.sunk | while | flops 685837312 | bytes 21023128 | solution.py:48
  24.9 0.9 compare_and_fusion.3
  25.8 0.9 fusion.65
  26.8 1.2 fusion.67
  27.9 1.1 fusion.66
  29.2 0.9 compare_and_fusion.3
  30.2 0.9 fusion.65
  31.1 1.2 fusion.67
  32.3 1.1 fusion.66
  33.4 0.1 divide_convert_fusion
  33.5 0.3 copy.34
  33.8 0.9 copy.60
  34.8 0.0 all-gather.8.cloned.1.call-start
  34.8 0.7 all-gather.8.cloned.1.call-update
  35.5 0.1 iota_compare_fusion.1
  35.6 0.1 iota_compare_fusion
  35.7 0.1 compare_and_fusion.1
  35.8 64.2 %all-gather.6.cloned.1.call-done = bf16[8192,128]{1,0:T(8,128)(2,1)} async-done(((bf16[128,128]{1,0:T(8,128)(2,1)}), bf16[8192,128]{1,0:T(8,128)(2,1)}) %all-gather.6.cloned.1.call-update) | async-done | bytes 2097168 | tf_op jit(solution)/shard_map/all_gather | solution.py:92
  99.9 40.7 %all-gather.4.cloned.1.call-done = bf16[256,8192]{1,0:T(8,128)(2,1)} async-done(((bf16[256,1024]{1,0:T(8,128)(2,1)}), bf16[256,8192]{1,0:T(8,128)(2,1)}) %all-gather.4.cloned.1.call-update) | async-done | bytes 4194320 | tf_op jit(solution)/shard_map/all_gather | solution.py:89
  140.6 4.1 fusion.48
  144.8 78.4 %all-gather.8.cloned.1.call-done = bf16[8192,128]{1,0:T(8,128)(2,1)} async-done(((bf16[128,128]{1,0:T(8,128)(2,1)}), bf16[8192,128]{1,0:T(8,128)(2,1)}) %all-gather.8.cloned.1.call-update) | async-done | bytes 2097168 | tf_op jit(solution)/shard_map/all_gather | solution.py:97
  223.1 4.1 fusion.49
  227.2 0.1 select_convert_fusion
  227.4 0.3 select_reduce_fusion
  227.7 0.2 bitcast_reduce_fusion
  227.9 113.3 %pmax.7 = f32[2,1,4,8]{3,2,0,1:T(4,128)S(1)} all-reduce(f32[2,1,4,8]{3,2,0,1:T(4,128)S(1)} %bitcast.153), channel_id=1, replica_groups=mesh['seq'=64,'head'=8] {'seq'}, use_global_device_ids=true, to_apply=%region_5.6 | all-reduce | flops 64 | bytes 512 | tf_op jit(solution)/shard_map/pmax | solution.py:130
  341.3 0.2 fusion.25
  341.5 219.7 %all-reduce = (f32[2,1,4,8,128]{4,3,2,0,1:T(8,128)S(1)}, f32[2,4,8]{2,1,0:T(4,128)S(1)}) all-reduce(f32[2,1,4,8,128]{4,3,2,0,1:T(8,128)S(1)} %fusion.25, f32[2,4,8]{2,1,0:T(4,128)S(1)} %get-tuple-element.101), channel_id=1, replica_groups=mesh['seq'=64,'head'=8] {'seq'}, use_global_device_ids=true, to_apply=%region_6.7 | all-reduce | flops 8256 | bytes 66048 | tf_op jit(solution)/shard_map/psum | solution.py:132
  561.2 0.1 fusion.41
  561.3 0.1 fusion.37
  561.5 98.6 %psum.23 = bf16[8,128]{1,0:T(8,128)(2,1)} all-reduce(f32[8,128]{1,0:T(8,128)S(1)} %fusion.37), channel_id=1, replica_groups=mesh['seq'=64,'head'=8] {'head'}, use_global_device_ids=true, to_apply=%region_9.10 | all-reduce | flops 1024 | bytes 6144 | tf_op jit(solution)/shard_map/psum | solution.py:140
  (39 shorter events, 0.3 us)
Async XLA Ops:
  7.2 554.2 %copy-start = (bf16[1024,128]{1,0:T(8,128)(2,1)S(1)}, bf16[1024,128]{1,0:T(8,128)(2,1)}, u32[]{:S(2)}) copy-start(bf16[1024,128]{1,0:T(8,128)(2,1)} %param.25) | copy-start | bytes 786436
  7.2 17.6 %copy-start.1 = (bf16[2,128,1,8,128]{4,3,2,1,0:T(8,128)(2,1)S(1)}, bf16[2,128,1,8,128]{4,3,2,1,0:T(8,128)(2,1)}, u32[]{:S(2)}) copy-start(bf16[2,128,1,8,128]{4,3,2,1,0:T(8,128)(2,1)} %param.19) | copy-start | bytes 1572868
  7.2 92.7 %all-gather.6.cloned.1.call-start = ((), (), s32[]{:S(2)}) async-start(), calls=%async_computation.1 | async-start | bytes 2129920 | tf_op jit(solution)/shard_map/all_gather | solution.py:92
  8.2 14.6 %collective-permute-start.1 = (bf16[2,256,1,128]{3,1,0,2:T(8,128)(2,1)S(1)}, bf16[2,256,1,128]{3,1,0,2:T(8,128)(2,1)}, u32[]{:S(2)}, u32[]{:S(2)}) collective-permute-start(bf16[2,256,1,128]{3,1,0,2:T(8,128)(2,1)S(1)} %slice.9), channel_id=1, source_target_pairs={{0,8},{8,16},{16,24},{24,32},{32,40},{40,48},{48,56},{56,64},{64,7... | collective-permute-start | bytes 393224 | tf_op jit(solution)/shard_map/ppermute | solution.py:18
  13.8 7.9 %collective-permute-start = (bf16[2,256,1,128]{3,1,0,2:T(8,128)(2,1)S(1)}, bf16[2,256,1,128]{3,1,0,2:T(8,128)(2,1)S(1)}, u32[]{:S(2)}, u32[]{:S(2)}) collective-permute-start(bf16[2,256,1,128]{3,1,0,2:T(8,128)(2,1)S(1)} %slice.8), channel_id=1, source_target_pairs={{0,8},{8,16},{16,24},{24,32},{32,40},{40,48},{48,56},{56,64},{64,7... | collective-permute-start | bytes 393224 | tf_op jit(solution)/shard_map/ppermute | solution.py:18
  16.4 124.2 %all-gather.4.cloned.1.call-start = ((), (), s32[]{:S(2)}) async-start(), calls=%async_computation | async-start | bytes 4718592 | tf_op jit(solution)/shard_map/all_gather | solution.py:89
  24.8 2.0 copy-start.2
  29.1 2.0 copy-start.2
  34.8 188.4 %all-gather.8.cloned.1.call-start = ((), (), s32[]{:S(2)}) async-start(), calls=%async_computation.2 | async-start | bytes 2129920 | tf_op jit(solution)/shard_map/all_gather | solution.py:97
  144.7 82.6 %copy-start.5 = (bf16[2,256,1,128]{3,1,2,0:T(8,128)(2,1)S(1)}, bf16[2,256,1,128]{3,1,2,0:T(8,128)(2,1)}, u32[]{:S(2)}) copy-start(bf16[2,256,1,128]{3,1,2,0:T(8,128)(2,1)} %param.22) | copy-start | bytes 393220
  144.8 82.6 %copy-start.7 = (bf16[4,2,1,8,128]{4,3,2,1,0:T(8,128)(2,1)S(1)}, bf16[4,2,1,8,128]{4,3,2,1,0:T(8,128)(2,1)}, u32[]{:S(2)}) copy-start(bf16[4,2,1,8,128]{4,3,2,1,0:T(8,128)(2,1)} %param.24) | copy-start | bytes 49156
  144.8 196.5 %copy-start.6 = (bf16[2,256,1,128]{3,1,2,0:T(8,128)(2,1)S(1)}, bf16[2,256,1,128]{3,1,2,0:T(8,128)(2,1)}, u32[]{:S(2)}) copy-start(bf16[2,256,1,128]{3,1,2,0:T(8,128)(2,1)} %param.23) | copy-start | bytes 393220
  227.4 432.7 %copy-start.3 = (bf16[2,128,1,128]{3,1,0,2:T(8,128)(2,1)}, bf16[2,128,1,128]{3,1,0,2:T(8,128)(2,1)S(1)}, u32[]{:S(2)}) copy-start(bf16[2,128,1,128]{3,1,0,2:T(8,128)(2,1)S(1)} %get-tuple-element.105) | copy-start | bytes 196612
  227.4 432.7 %copy-start.4 = (bf16[2,128,1,128]{3,1,0,2:T(8,128)(2,1)}, bf16[2,128,1,128]{3,1,0,2:T(8,128)(2,1)S(1)}, u32[]{:S(2)}) copy-start(bf16[2,128,1,128]{3,1,0,2:T(8,128)(2,1)S(1)} %get-tuple-element.106) | copy-start | bytes 196612
Sparse Core Ops, SparseCore 0:
  16.6 83.3 all-gather.5
  102.0 38.5 all-gather.3
  143.7 79.3 all-gather.7
where the time goes:
time: 667 us
  blocking collectives  432 us (65%)
  waiting for transfers between devices  184 us (28%)
  between operations  14 us (2%)
  matrix products  13.1 us (2%)
  other arithmetic  10.8 us (2%)
  starting transfers between devices  7.38 us (1%)
    psum x1, blocking collectives, body(): lax.psum((weight_sum * rescale, weighted * rescale[..., None]), 'seq')  220 us
    pmax x1, blocking collectives, body(): global_peak = lax.pmax(row_peak, 'seq')  113 us
    psum x1, blocking collectives, body(): summed = lax.psum(partial_value, 'head')  98.6 us
    all_gather x1, waiting for transfers between devices, body(): lax.all_gather(beacon_wv, 'seq', axis=0, tiled=True)  78.4 us
    all_gather x1, waiting for transfers between devices, body(): lax.all_gather(beacon_wk, 'seq', axis=0, tiled=True)  64.2 us
    all_gather x1, waiting for transfers between devices, body(): pooled_whole = lax.all_gather(pooled_flat, 'head', axis=1, tiled=True)  40.7 us
  transfers between devices with their start and end apart: 5, of which 3 were waited for; matrix products, arithmetic and copies ran while one was open for 3% of the time, Pallas kernels for 0%

commit v1 on v0

--- a/solution.py
+++ b/solution.py
@@ -10,6 +10,16 @@
 OFF = 256
 STEPS = 4
 masked_score = -1e30
+
+
+def pass_along(x, name, dim):
+    size = lax.axis_size(name)
+    moving, parts = (x, [x])
+    for _ in range(size - 1):
+        moving = lax.ppermute(moving, name, [(i, (i + 1) % size) for i in range(size)])
+        parts.insert(0, moving)
+    merged = jnp.concatenate(parts, axis=dim)
+    return jnp.roll(merged, (lax.axis_index(name) + 1) * x.shape[dim], axis=dim)
 
 
 def shifted(value, axis, steps):
@@ -86,7 +96,7 @@
     pooled_parts = pool_part(beacon_queries, key_rows, value_rows, positions, present, reaches)
     pooled = (pooled_parts[2] / pooled_parts[1][..., None]).astype(jnp.bfloat16)
     pooled_flat = pooled.reshape(requests * NB, kv_local * G * head_dim)
-    pooled_whole = lax.all_gather(pooled_flat, "head", axis=1, tiled=True)
+    pooled_whole = pass_along(pooled_flat, "head", 1)
     key_sum = jnp.dot(
         pooled_whole,
         lax.all_gather(beacon_wk, "seq", axis=0, tiled=True),

time: 667 us -> 628 us (0.942)
  waiting for transfers between devices: 184 us -> 113 us
  starting transfers between devices: 7.38 us -> 23.3 us
  local copies, waits for them, and re-layouts: 5.63 us -> 21.4 us
    all_gather x1, waiting for transfers between devices: 64.2 us -> 0.01 us  [body(): lax.all_gather(beacon_wk, 'seq', axis=0, tiled=True)]
    ppermute x0 -> x7, waiting for transfers between devices: none -> 46.7 us  [pass_along(): lax.ppermute(moving, name, [(i, (i + 1) % size) for i in range(size)])]
    all_gather x1 -> x0, waiting for transfers between devices: 40.7 us -> none  [body(): pooled_whole = lax.all_gather(pooled_flat, 'head', axis=1, tiled=True)]
    ppermute x0 -> x7, starting transfers between devices: none -> 15.9 us  [pass_along(): lax.ppermute(moving, name, [(i, (i + 1) % size) for i in range(size)])]
    unnamed x16 -> x33, local copies, waits for them, and re-layouts: 2.24 us -> 16.2 us
    all_gather x1, waiting for transfers between devices: 78.4 us -> 66.7 us  [body(): lax.all_gather(beacon_wv, 'seq', axis=0, tiled=True)]
  transfers between devices with their start and end apart: 5 -> 11, of which waited for: 3 -> 8; matrix products, arithmetic and copies ran while one was open for 3% -> 6% of each run, Pallas kernels for 0% -> 0%
where the time goes in v1:
time: 628 us; the launch traced here: 627 us
  blocking collectives  432 us (69%)
  waiting for transfers between devices  113 us (18%)
  starting transfers between devices  23.3 us (4%)
  local copies, waits for them, and re-layouts  21.4 us (3%)
  between operations  14.3 us (2%)
  matrix products  13.1 us (2%)
  other arithmetic  9.99 us (2%)
    psum x1, blocking collectives, body(): lax.psum((weight_sum * rescale, weighted * rescale[..., None]), 'seq')  220 us
    pmax x1, blocking collectives, body(): global_peak = lax.pmax(row_peak, 'seq')  113 us
    psum x1, blocking collectives, body(): summed = lax.psum(partial_value, 'head')  98.6 us
    all_gather x1, waiting for transfers between devices, body(): lax.all_gather(beacon_wv, 'seq', axis=0, tiled=True)  66.7 us
    ppermute x7, waiting for transfers between devices, pass_along(): lax.ppermute(moving, name, [(i, (i + 1) % size) for i in range(size)])  46.7 us
    unnamed x33, local copies, waits for them, and re-layouts  16.2 us
    ppermute x7, starting transfers between devices, pass_along(): lax.ppermute(moving, name, [(i, (i + 1) % size) for i in range(size)])  15.9 us
  transfers between devices with their start and end apart: 11, of which 8 were waited for; matrix products, arithmetic and copies ran while one was open for 6% of the time, Pallas kernels for 0%

profile of v1, /device:TPU:1, one launch (start us, length us, event | category | flops | bytes accessed | tf_op | source)
XLA Modules:
  0.0 627.2 jit_solution(12281752857547268177)
XLA Ops:
  7.2 1.0 slice.9
  8.2 4.0 collective-permute-start.1
  12.2 0.9 slice.8
  13.2 3.2 collective-permute-start
  17.9 1.2 copy.32
  20.6 1.0 fusion.48
  21.7 1.1 pad_maximum_fusion
  23.0 10.5 %while.12 = (s32[]{:T(128)}, f32[2,128,1,8]{1,3,2,0:T(8,128)S(1)}, f32[2,128,1,8,128]{1,4,3,2,0:T(8,128)S(1)}, pred[2,1280]{1,0:T(4,128)(4,1)S(1)}, s32[2,1280]{...) while((s32[]{:T(128)}, f32[2,128,1,8]{1,3,2,0:T(8,128)S(1)}, ...), condition=%wide.region_3.4_spmd, body=%wide.region_0.3_spmd.sunk | while | flops 685837312 | bytes 18401660 | solution.py:58
  23.1 0.9 compare_and_fusion.3
  24.1 1.0 constant_dynamic-slice_fusion.4
  25.0 0.9 fusion.68
  25.9 1.2 fusion.70
  27.1 1.1 fusion.69
  28.3 0.9 compare_and_fusion.3
  29.3 1.0 constant_dynamic-slice_fusion.4
  30.3 0.9 fusion.68
  31.2 1.2 fusion.70
  32.4 1.1 fusion.69
  34.0 2.3 collective-permute-start.2
  36.4 6.1 collective-permute-done.2
  42.5 2.5 collective-permute-start.3
  45.0 6.1 collective-permute-done.3
  51.1 2.5 collective-permute-start.4
  53.6 6.1 collective-permute-done.4
  59.7 2.5 collective-permute-start.5
  62.2 6.1 collective-permute-done.5
  68.3 2.5 collective-permute-start.6
  70.8 6.1 collective-permute-done.6
  76.9 2.5 collective-permute-start.7
  79.5 7.4 %collective-permute-done.7 = bf16[256,1024]{1,0:T(8,128)(2,1)} collective-permute-done((bf16[256,1024]{1,0:T(8,128)(2,1)S(1)}, bf16[256,1024]{1,0:T(8,128)(2,1)}, u32[]{:S(2)}, u32[]{:S(2)}) %collective-permute-start.7) | collective-permute-done | bytes 524320 | tf_op jit(solution)/shard_map/ppermute | solution.py:19
  86.9 1.2 collective-permute-start.8
  88.3 8.6 %collective-permute-done.8 = bf16[256,1024]{1,0:T(8,128)(2,1)S(1)} collective-permute-done((bf16[256,1024]{1,0:T(8,128)(2,1)}, bf16[256,1024]{1,0:T(8,128)(2,1)S(1)}, u32[]{:S(2)}, u32[]{:S(2)}) %collective-permute-start.8) | collective-permute-done | bytes 524320 | tf_op jit(solution)/shard_map/ppermute | solution.py:19
  96.9 0.9 constant_dynamic-update-slice_fusion.15
  97.8 1.9 constant_dynamic-update-slice_fusion.14
  99.7 0.9 constant_dynamic-update-slice_fusion.13
  100.5 0.9 constant_dynamic-update-slice_fusion.12
  103.0 0.9 constant_dynamic-update-slice_fusion.9
  103.9 0.9 constant_dynamic-update-slice_fusion.8
  105.6 1.9 constant_dynamic-update-slice_fusion.6
  108.4 0.9 constant_dynamic-update-slice_fusion.4
  110.9 0.9 constant_dynamic-update-slice_fusion.1
  111.7 0.9 constant_dynamic-update-slice_fusion
  112.6 4.1 fusion.27
  116.7 66.7 %all-gather.5.cloned.1.call-done = bf16[8192,128]{1,0:T(8,128)(2,1)} async-done(((bf16[128,128]{1,0:T(8,128)(2,1)}), bf16[8192,128]{1,0:T(8,128)(2,1)}) %all-gather.5.cloned.1.call-update) | async-done | bytes 2097168 | tf_op jit(solution)/shard_map/all_gather | solution.py:107
  183.4 4.1 fusion.25
  188.2 113.3 %pmax.7 = f32[2,1,4,8]{3,2,0,1:T(4,128)S(1)} all-reduce(f32[2,1,4,8]{3,2,0,1:T(4,128)S(1)} %bitcast.157), channel_id=1, replica_groups=mesh['seq'=64,'head'=8] {'seq'}, use_global_device_ids=true, to_apply=%region_5.6 | all-reduce | flops 64 | bytes 512 | tf_op jit(solution)/shard_map/pmax | solution.py:140
  301.8 219.7 %all-reduce = (f32[2,1,4,8,128]{4,3,2,0,1:T(8,128)S(1)}, f32[2,4,8]{2,1,0:T(4,128)S(1)}) all-reduce(f32[2,1,4,8,128]{4,3,2,0,1:T(8,128)S(1)} %fusion.29, f32[2,4,8]{2,1,0:T(4,128)S(1)} %get-tuple-element.101), channel_id=1, replica_groups=mesh['seq'=64,'head'=8] {'seq'}, use_global_device_ids=true, to_apply=%region_6.7 | all-reduce | flops 8256 | bytes 66048 | tf_op jit(solution)/shard_map/psum | solution.py:142
  521.8 98.6 %psum.23 = bf16[8,128]{1,0:T(8,128)(2,1)} all-reduce(f32[8,128]{1,0:T(8,128)S(1)} %fusion.41), channel_id=1, replica_groups=mesh['seq'=64,'head'=8] {'head'}, use_global_device_ids=true, to_apply=%region_9.10 | all-reduce | flops 1024 | bytes 6144 | tf_op jit(solution)/shard_map/psum | solution.py:150
  (64 shorter events, 10.3 us)
Async XLA Ops:
  7.2 514.4 %copy-start = (bf16[1024,128]{1,0:T(8,128)(2,1)S(1)}, bf16[1024,128]{1,0:T(8,128)(2,1)}, u32[]{:S(2)}) copy-start(bf16[1024,128]{1,0:T(8,128)(2,1)} %param.25) | copy-start | bytes 786436
  7.2 105.5 %all-gather.3.cloned.1.call-start = ((), (), s32[]{:S(2)}) async-start(), calls=%async_computation | async-start | bytes 2129920 | tf_op jit(solution)/shard_map/all_gather | solution.py:102
  8.2 14.6 %collective-permute-start.1 = (bf16[2,256,1,128]{3,1,0,2:T(8,128)(2,1)S(1)}, bf16[2,256,1,128]{3,1,0,2:T(8,128)(2,1)S(1)}, u32[]{:S(2)}, u32[]{:S(2)}) collective-permute-start(bf16[2,256,1,128]{3,1,0,2:T(8,128)(2,1)S(1)} %slice.9), channel_id=1, source_target_pairs={{0,8},{8,16},{16,24},{24,32},{32,40},{40,48},{48,56},{56,64},{64,7... | collective-permute-start | bytes 393224 | tf_op jit(solution)/shard_map/ppermute | solution.py:28
  13.2 8.6 %copy-start.1 = (bf16[2,256,1,128]{3,1,0,2:T(8,128)(2,1)}, bf16[2,256,1,128]{3,1,0,2:T(8,128)(2,1)S(1)}, u32[]{:S(2)}) copy-start(bf16[2,256,1,128]{3,1,0,2:T(8,128)(2,1)S(1)} %slice.8) | copy-start | bytes 393220
  13.2 8.6 %collective-permute-start = (bf16[2,256,1,128]{3,1,0,2:T(8,128)(2,1)S(1)}, bf16[2,256,1,128]{3,1,0,2:T(8,128)(2,1)S(1)}, u32[]{:S(2)}, u32[]{:S(2)}) collective-permute-start(bf16[2,256,1,128]{3,1,0,2:T(8,128)(2,1)S(1)} %slice.8), channel_id=1, source_target_pairs={{0,8},{8,16},{16,24},{24,32},{32,40},{40,48},{48,56},{56,64},{64,7... | collective-permute-start | bytes 393224 | tf_op jit(solution)/shard_map/ppermute | solution.py:28
  16.4 167.0 %all-gather.5.cloned.1.call-start = ((), (), s32[]{:S(2)}) async-start(), calls=%async_computation.1 | async-start | bytes 2129920 | tf_op jit(solution)/shard_map/all_gather | solution.py:107
  34.0 8.5 %collective-permute-start.2 = (bf16[256,1024]{1,0:T(8,128)(2,1)S(1)}, bf16[256,1024]{1,0:T(8,128)(2,1)S(1)}, u32[]{:S(2)}, u32[]{:S(2)}) collective-permute-start(bf16[256,1024]{1,0:T(8,128)(2,1)S(1)} %bitcast.150), channel_id=1, source_target_pairs={{0,1},{1,2},{2,3},{3,4},{4,5},{5,6},{6,7},{7,0},{8,9},{9,10},{10,1... | collective-permute-start | bytes 1572872 | tf_op jit(solution)/shard_map/ppermute | solution.py:19
  42.5 8.6 %collective-permute-start.3 = (bf16[256,1024]{1,0:T(8,128)(2,1)S(1)}, bf16[256,1024]{1,0:T(8,128)(2,1)S(1)}, u32[]{:S(2)}, u32[]{:S(2)}) collective-permute-start(bf16[256,1024]{1,0:T(8,128)(2,1)S(1)} %collective-permute-done.2), channel_id=1, source_target_pairs={{0,1},{1,2},{2,3},{3,4},{4,5},{5,6},{6,7},{7,0},{8,9},{9,10},{10,1... | collective-permute-start | bytes 1572872 | tf_op jit(solution)/shard_map/ppermute | solution.py:19
  51.1 8.6 %collective-permute-start.4 = (bf16[256,1024]{1,0:T(8,128)(2,1)S(1)}, bf16[256,1024]{1,0:T(8,128)(2,1)S(1)}, u32[]{:S(2)}, u32[]{:S(2)}) collective-permute-start(bf16[256,1024]{1,0:T(8,128)(2,1)S(1)} %collective-permute-done.3), channel_id=1, source_target_pairs={{0,1},{1,2},{2,3},{3,4},{4,5},{5,6},{6,7},{7,0},{8,9},{9,10},{10,1... | collective-permute-start | bytes 1572872 | tf_op jit(solution)/shard_map/ppermute | solution.py:19
  59.7 8.6 %collective-permute-start.5 = (bf16[256,1024]{1,0:T(8,128)(2,1)S(1)}, bf16[256,1024]{1,0:T(8,128)(2,1)S(1)}, u32[]{:S(2)}, u32[]{:S(2)}) collective-permute-start(bf16[256,1024]{1,0:T(8,128)(2,1)S(1)} %collective-permute-done.4), channel_id=1, source_target_pairs={{0,1},{1,2},{2,3},{3,4},{4,5},{5,6},{6,7},{7,0},{8,9},{9,10},{10,1... | collective-permute-start | bytes 1572872 | tf_op jit(solution)/shard_map/ppermute | solution.py:19
  68.3 8.6 %collective-permute-start.6 = (bf16[256,1024]{1,0:T(8,128)(2,1)S(1)}, bf16[256,1024]{1,0:T(8,128)(2,1)S(1)}, u32[]{:S(2)}, u32[]{:S(2)}) collective-permute-start(bf16[256,1024]{1,0:T(8,128)(2,1)S(1)} %collective-permute-done.5), channel_id=1, source_target_pairs={{0,1},{1,2},{2,3},{3,4},{4,5},{5,6},{6,7},{7,0},{8,9},{9,10},{10,1... | collective-permute-start | bytes 1572872 | tf_op jit(solution)/shard_map/ppermute | solution.py:19
  76.9 9.9 %collective-permute-start.7 = (bf16[256,1024]{1,0:T(8,128)(2,1)S(1)}, bf16[256,1024]{1,0:T(8,128)(2,1)}, u32[]{:S(2)}, u32[]{:S(2)}) collective-permute-start(bf16[256,1024]{1,0:T(8,128)(2,1)S(1)} %collective-permute-done.6), channel_id=1, source_target_pairs={{0,1},{1,2},{2,3},{3,4},{4,5},{5,6},{6,7},{7,0},{8,9},{9,10},{10,1... | collective-permute-start | bytes 1572872 | tf_op jit(solution)/shard_map/ppermute | solution.py:19
  86.9 10.0 %collective-permute-start.8 = (bf16[256,1024]{1,0:T(8,128)(2,1)}, bf16[256,1024]{1,0:T(8,128)(2,1)S(1)}, u32[]{:S(2)}, u32[]{:S(2)}) collective-permute-start(bf16[256,1024]{1,0:T(8,128)(2,1)} %collective-permute-done.7), channel_id=1, source_target_pairs={{0,1},{1,2},{2,3},{3,4},{4,5},{5,6},{6,7},{7,0},{8,9},{9,10},{10,1... | collective-permute-start | bytes 1572872 | tf_op jit(solution)/shard_map/ppermute | solution.py:19
  109.2 78.4 %copy-start.2 = (bf16[2,256,1,128]{3,1,0,2:T(8,128)(2,1)S(1)}, bf16[2,256,1,128]{3,1,0,2:T(8,128)(2,1)}, u32[]{:S(2)}) copy-start(bf16[2,256,1,128]{3,1,0,2:T(8,128)(2,1)} %copy-done.1) | copy-start | bytes 393220
  109.2 78.5 %copy-start.5 = (bf16[2,256,1,128]{3,1,2,0:T(8,128)(2,1)S(1)}, bf16[2,256,1,128]{3,1,2,0:T(8,128)(2,1)}, u32[]{:S(2)}) copy-start(bf16[2,256,1,128]{3,1,2,0:T(8,128)(2,1)} %param.22) | copy-start | bytes 393220
  109.2 78.5 %copy-start.7 = (bf16[4,2,1,8,128]{4,3,2,1,0:T(8,128)(2,1)S(1)}, bf16[4,2,1,8,128]{4,3,2,1,0:T(8,128)(2,1)}, u32[]{:S(2)}) copy-start(bf16[4,2,1,8,128]{4,3,2,1,0:T(8,128)(2,1)} %param.24) | copy-start | bytes 49156
  110.9 190.7 %copy-start.6 = (bf16[2,256,1,128]{3,1,2,0:T(8,128)(2,1)S(1)}, bf16[2,256,1,128]{3,1,2,0:T(8,128)(2,1)}, u32[]{:S(2)}) copy-start(bf16[2,256,1,128]{3,1,2,0:T(8,128)(2,1)} %param.23) | copy-start | bytes 393220
  187.6 432.7 %copy-start.3 = (bf16[2,128,1,128]{3,1,0,2:T(8,128)(2,1)}, bf16[2,128,1,128]{3,1,0,2:T(8,128)(2,1)S(1)}, u32[]{:S(2)}) copy-start(bf16[2,128,1,128]{3,1,0,2:T(8,128)(2,1)S(1)} %get-tuple-element.105) | copy-start | bytes 196612
  187.7 432.7 %copy-start.4 = (bf16[2,128,1,128]{3,1,0,2:T(8,128)(2,1)}, bf16[2,128,1,128]{3,1,0,2:T(8,128)(2,1)S(1)}, u32[]{:S(2)}) copy-start(bf16[2,128,1,128]{3,1,0,2:T(8,128)(2,1)S(1)} %get-tuple-element.106) | copy-start | bytes 196612
Sparse Core Ops, SparseCore 0:
  16.5 83.1 all-gather.2
  102.8 80.5 all-gather.4
